TPU v7x, 128 devices: a whole 4x4x4 slice. The times are simulated.
128 devices in a mesh: row: 4 (over y), col: 32 (over x, z, core).
Axes of the slice: x: 4, y: 4, z: 4, core: 2. Of those that a mesh axis runs over, the one named last changes fastest.
Arguments:
- template: float32 [2048, 8192], P('row', 'col')
- template_var: float32 [2048, 8192], P('row', 'col'), may hold values from 0.1 to 1
- coverage: int32 [2048, 8192], P('row', 'col'), may hold values 0 or 1
- exposure: float32 [4, 4096, 4, 256], P('row', 'col')
- exposure_var: float32 [4, 4096, 4, 256], P('row', 'col'), may hold values from 0.25 to 4
- strip_owner: int32 [4, 4096], P('row', 'col'), may hold values from 0 to 127, as said below
- strip_slot: int32 [4, 4096], P('row', 'col'), may hold values from 0 to 127, as said below
Outputs:
- difference: float32 [2048, 8192], P('row', 'col')
- variance: float32 [2048, 8192], P('row', 'col')
Inputs may be any that keep to these rules, and one draw needn't show every extreme that they name: `strip_owner`: over all devices, every (owner, position) pair is named by exactly one block. Each device sends exactly 1 block to every owner. `strip_slot`: together with strip_owner, a permutation of all owned row blocks; all blocks of one device take the same position at their owners.
All inputs are finite; a program needn't handle non-finite values. No bound on the sum of `coverage` on one device may be relied on, other than what follows from the above.
Results may differ from a plain program's by a relative error of at most 0.0056.
Values may be sent and summed in bfloat16 or wider, within the bound.
A program may use at most 128 MiB of HBM per device.

v0:
```python
import jax
import jax.numpy as jnp
import numpy as np
from jax import lax
from jax.experimental import pallas as pl
from jax.experimental.pallas import tpu as pltpu
from jax.sharding import PartitionSpec as P

RIDGE = 0.05
SIGMAS = (1.0, 2.0, 4.0)
MESH = pl.DeviceIdType.MESH
F32 = jnp.float32
BF16 = jnp.bfloat16

SLOTS = (
    (0, 0), (0, 2), (1, 0), (1, 2), (2, 0), (2, 2), (0, 1), (1, 1),
    (2, 1), (0, 3), (1, 3), None, (2, 3), (0, 4), (1, 4), (2, 4),
)
GROUP_OF_PASS = (0, 1, 2, 3, 4, 4, 5, 5)
BLOCK = 96
TARGET = 47
DIRECTIONS = ((0, -1), (0, 1), (-1, 0), (1, 0), (-1, -1), (-1, 1), (1, -1), (1, 1))


def filter_bank():
    taps = np.arange(31) - 15.0
    collected = []
    for sigma in SIGMAS:
        for degree in range(5):
            scaled = taps / sigma
            shape = scaled**degree * np.exp(-0.5 * scaled * scaled)
            collected.append(shape / np.sqrt(np.sum(shape * shape)))
    return np.array(collected, np.float32).astype(jnp.bfloat16).astype(np.float32)


def tables():
    bank = filter_bank()
    x_weights = np.zeros((8, 256, 2, 128), np.float32)
    y_weights = np.zeros((8, BLOCK, 8, 2, 128), np.float32)
    across = np.arange(128)
    down = np.arange(BLOCK)
    order = []
    filled = [0] * 6
    for number, slot in enumerate(SLOTS):
        if slot is None:
            continue
        half, which = number // 2, number % 2
        s, i = slot
        group = GROUP_OF_PASS[half]
        for q in range(31):
            x_weights[half, across + q - 15 + 64, which, across] = bank[s * 5 + i, q]
        for j in range(5 - i):
            lane = filled[group]
            filled[group] += 1
            order.append((group * 8 + lane, s, i, j))
            for p in range(31):
                y_weights[half, down, lane, which, down + p - 15 + 16] = bank[s * 5 + j, p]
    shapes = np.zeros((48, 31 * 31), np.float64)
    for t, s, i, j in order:
        shapes[t] = np.outer(bank[s * 5 + j], bank[s * 5 + i]).reshape(-1).astype(np.float64)
    values, vectors = np.linalg.eigh(shapes @ shapes.T)
    root = np.sqrt(np.maximum(values, 0.0))[:, None] * vectors.T
    power = np.zeros((48, 128), np.float32)
    power[:, :48] = root
    power[:, 64:112] = root
    spread = np.zeros((2, 128, 768), np.float32)
    for patch in range(2):
        spread[patch, 64 * patch + np.arange(768) % 48, np.arange(768)] = 1.0
    return (
        x_weights.reshape(8, 256, 256).astype(jnp.bfloat16),
        y_weights.reshape(8, BLOCK * 8, 256).astype(jnp.bfloat16),
        power,
        spread.astype(jnp.bfloat16),
    )


def inverse_row(columns, size=128):
    rows = lax.broadcasted_iota(jnp.int32, (size, size), 0)
    lanes = lax.broadcasted_iota(jnp.int32, (size, size), 1)
    return jnp.max(jnp.where(columns == lanes, rows, 0), 0, keepdims=True)


def within(number):
    return jnp.clip(number, 0, 127)


def kernel(
    template, template_var, coverage, flux, noise, owner, slot, x_weights, y_weights, power, spread,
    difference, variance,
    wide, filtered, conv, send, recv, labels, science, science_var, root, own_gram, near_gram,
    row_index, table_in, table_out,
    halo_out, halo_in, part_out, part_in, label_out, label_in, gram_out, gram_in,
):
    r = lax.axis_index("row")
    c = lax.axis_index("col")
    x, z, k = c // 8, (c // 2) % 4, c % 2
    me = r * 32 + c
    place = (z * 2 + k) * 16 + r * 4 + x
    barrier = pltpu.get_barrier_semaphore()

    wide[...] = jnp.zeros_like(wide)
    near_gram[...] = jnp.zeros_like(near_gram)

    def greet(step, carry):
        other = lax.rem(me + step, 128)
        pl.semaphore_signal(barrier, inc=1, device_id=(other // 32, other % 32), device_id_type=MESH)
        return carry

    lax.fori_loop(1, 128, greet, 0)

    wide[16:528, 128:384] = template[...].astype(BF16)
    labels[pl.ds(place, 1), :] = slot[...]
    columns = jnp.transpose(jnp.broadcast_to(owner[...], (128, 128)))
    row_index[...] = jnp.broadcast_to(inverse_row(columns), (8, 128))
    pltpu.sync_copy(row_index, table_in)

    def pack(number, carry):
        block = within(table_in[0, number])
        send[number] = jnp.concatenate([flux[block], noise[block]], 0).astype(BF16)
        return carry

    lax.fori_loop(0, 128, pack, 0, unroll=4)
    recv[place] = send[me]
    filtered[:, 544:608, :] = jnp.zeros((16, 64, 256), BF16)
    pl.semaphore_wait(barrier, 127)

    def inside(dr, dc):
        return jnp.logical_and(
            jnp.logical_and(r + dr >= 0, r + dr < 4), jnp.logical_and(c + dc >= 0, c + dc < 32)
        )

    def target(dr, dc):
        return (jnp.clip(r + dr, 0, 3), jnp.clip(c + dc, 0, 31))

    source_rows = {-1: pl.ds(16, 16), 0: pl.ds(16, 512), 1: pl.ds(512, 16)}
    target_rows = {-1: pl.ds(528, 16), 0: pl.ds(16, 512), 1: pl.ds(0, 16)}
    source_cols = {-1: pl.ds(128, 128), 0: pl.ds(128, 256), 1: pl.ds(256, 128)}
    target_cols = {-1: pl.ds(384, 128), 0: pl.ds(128, 256), 1: pl.ds(0, 128)}

    def halo(number):
        dr, dc = DIRECTIONS[number]
        return pltpu.make_async_remote_copy(
            src_ref=wide.at[source_rows[dr], source_cols[dc]],
            dst_ref=wide.at[target_rows[dr], target_cols[dc]],
            send_sem=halo_out.at[number],
            recv_sem=halo_in.at[number],
            device_id=target(dr, dc),
            device_id_type=MESH,
        )

    def gram_copy(number):
        dr, dc = DIRECTIONS[number]
        return pltpu.make_async_remote_copy(
            src_ref=own_gram,
            dst_ref=near_gram.at[number],
            send_sem=gram_out.at[number],
            recv_sem=gram_in.at[number],
            device_id=target(dr, dc),
            device_id_type=MESH,
        )

    def each_sent(make, action):
        for number, (dr, dc) in enumerate(DIRECTIONS):
            @pl.when(inside(dr, dc))
            def _():
                action(make(number))

    def each_received(make):
        for number, (dr, dc) in enumerate(DIRECTIONS):
            @pl.when(inside(-dr, -dc))
            def _():
                make(number).wait_recv()

    each_sent(halo, lambda copy: copy.start())

    def label_copy(first, count, row, col, which):
        return pltpu.make_async_remote_copy(
            src_ref=labels.at[pl.ds(first, count)],
            dst_ref=labels.at[pl.ds(first, count)],
            send_sem=label_out.at[which],
            recv_sem=label_in.at[which],
            device_id=(row, col),
            device_id_type=MESH,
        )

    for dr in range(4):
        for dx in range(4):
            if dr or dx:
                label_copy(place, 1, (r + dr) % 4, ((x + dx) % 4) * 8 + z * 2 + k, 0).start()

    def send_part(step, carry):
        other = lax.rem(me + step, 128)
        pltpu.make_async_remote_copy(
            src_ref=send.at[other],
            dst_ref=recv.at[place],
            send_sem=part_out,
            recv_sem=part_in,
            device_id=(other // 32, other % 32),
            device_id_type=MESH,
        ).start()
        return carry

    lax.fori_loop(1, 128, send_part, 0)

    each_received(halo)

    whole = wide[...]
    windows = (whole[:, 64:320], whole[:, 192:448])

    def along_x(half, carry):
        for side in range(2):
            product = jnp.dot(windows[side], x_weights[half], preferred_element_type=F32).astype(BF16)
            for which in range(2):
                filtered[2 * half + which, 0:544, side * 128 : side * 128 + 128] = product[
                    :, which * 128 : which * 128 + 128
                ]
        return carry

    lax.fori_loop(0, 8, along_x, 0)

    def label_wait(count, which):
        part = labels.at[pl.ds(0, count)]
        pltpu.make_async_copy(part, part, label_in.at[which]).wait()
        pltpu.make_async_copy(part, part, label_out.at[which]).wait()

    label_wait(15, 0)
    for dz in range(4):
        for dk in range(2):
            if dz or dk:
                label_copy(
                    pl.multiple_of((z * 2 + k) * 16, 16), 16, r, x * 8 + ((z + dz) % 4) * 2 + (k + dk) % 2, 1
                ).start()

    def along_y(first, rows):
        for pair in range(3):
            groups = []
            for group in (2 * pair, 2 * pair + 1):
                total = None
                for half in range(8):
                    if GROUP_OF_PASS[half] == group:
                        window = filtered[2 * half : 2 * half + 2, pl.ds(first, 128), :].reshape(256, 256)
                        product = jnp.dot(
                            y_weights[half, 0 : rows * 8, :], window, preferred_element_type=F32
                        )
                        total = product if total is None else total + product
                groups.append(total.reshape(rows, 8, 256))
            conv[pl.ds(first, rows), pair * 16 : pair * 16 + 16, :] = jnp.concatenate(groups, 1).astype(BF16)

    def y_block(number, carry):
        along_y(pl.multiple_of(number * BLOCK, 16), BLOCK)
        return carry

    lax.fori_loop(0, 5, y_block, 0)
    along_y(480, 32)

    label_wait(112, 1)
    row_index[...] = jnp.broadcast_to(inverse_row(labels[...]), (8, 128))
    pltpu.sync_copy(row_index, table_out)
    parts = recv.at[pl.ds(0, 127)]
    pltpu.make_async_copy(parts, parts, part_in).wait()
    pltpu.make_async_copy(parts, parts, part_out).wait()

    def unpack(number, carry):
        upper = recv[within(table_out[0, 2 * number])].astype(F32)
        lower = recv[within(table_out[0, 2 * number + 1])].astype(F32)
        rows = pl.ds(pl.multiple_of(number * 8, 8), 8)
        science[rows, 0:128] = jnp.concatenate([upper[0:4], lower[0:4]], 0)
        science[rows, 128:256] = jnp.concatenate([upper[4:8], lower[4:8]], 0)
        science_var[rows, 0:128] = jnp.concatenate([upper[8:12], lower[8:12]], 0)
        science_var[rows, 128:256] = jnp.concatenate([upper[12:16], lower[12:16]], 0)
        return carry

    lax.fori_loop(0, 64, unpack, 0, unroll=4)
    root[...] = coverage[...].astype(F32) * lax.rsqrt(science_var[...])

    is_target = lax.broadcasted_iota(jnp.int32, (16, 256), 0) == TARGET - 32

    def gram_rows(number, total):
        base = pl.multiple_of(number * 8, 8)
        pieces = []
        for row in range(8):
            weight = root[pl.ds(base + row, 1), :]
            goal = weight * science[pl.ds(base + row, 1), :]
            basis = conv[base + row].astype(F32) * weight
            last = jnp.where(is_target, goal, basis[32:48])
            pieces.append(jnp.concatenate([basis[0:32].astype(BF16), last.astype(BF16)], 0))
        block = jnp.concatenate(pieces, 1)
        return total + lax.dot_general(
            block, block, (((1,), (1,)), ((), ())), preferred_element_type=F32
        )

    own_gram[...] = jnp.zeros_like(own_gram)
    for patch in range(2):
        total = lax.fori_loop(32 * patch, 32 * patch + 32, gram_rows, jnp.zeros((48, 48), F32))
        own_gram[:, patch * 64 : patch * 64 + 48] = total

    each_sent(gram_copy, lambda copy: copy.start())
    each_received(gram_copy)

    lane = lax.broadcasted_iota(jnp.int32, (48, 128), 1)
    sub = lax.broadcasted_iota(jnp.int32, (48, 128), 0)
    beside = own_gram[...] + near_gram[0] + near_gram[1]
    from_below = near_gram[2] + near_gram[4] + near_gram[5]
    from_above = near_gram[3] + near_gram[6] + near_gram[7]
    moved = beside + jnp.where(lane < 64, from_below, from_above)
    system = beside + pltpu.roll(moved, 64, 1)
    half_lane = lane % 64
    diagonal = jnp.logical_and(sub == half_lane, sub < 45)
    on_diagonal = jnp.where(diagonal, system, 0.0)
    trace_upper = jnp.sum(jnp.where(lane < 64, on_diagonal, 0.0))
    trace_lower = jnp.sum(jnp.where(lane < 64, 0.0, on_diagonal))
    ridge = jnp.where(lane < 64, trace_upper, trace_lower) * (RIDGE / 45.0)
    system = jnp.where(diagonal, system + ridge, system)

    def eliminate(step, system):
        pivot_row = jnp.sum(jnp.where(sub == step, system, 0.0), 0, keepdims=True)
        pick = (lane - half_lane) + step
        column = jnp.take_along_axis(system, pick, axis=1)
        pivot = jnp.sum(jnp.where(sub == step, column, 0.0), 0, keepdims=True)
        scaled = column * (1.0 / pivot)
        return jnp.where(half_lane == step, scaled, system - scaled * pivot_row)

    system = lax.fori_loop(0, 45, eliminate, system)
    answer = jnp.where(jnp.logical_and(half_lane[47:48] < 45, lane[47:48] < 128), system[TARGET : TARGET + 1], 0.0)
    terms = power[...] * answer
    upper_terms = jnp.sum(jnp.where(lane < 64, terms, 0.0), 1, keepdims=True)
    lower_terms = jnp.sum(jnp.where(lane < 64, 0.0, terms), 1, keepdims=True)
    powers = (jnp.sum(upper_terms * upper_terms), jnp.sum(lower_terms * lower_terms))

    coarse = answer.astype(BF16)
    fine = (answer - coarse.astype(F32)).astype(BF16)
    row_of = lax.broadcasted_iota(jnp.int32, (32, 768), 0)
    lane_of = lax.broadcasted_iota(jnp.int32, (32, 768), 1)
    chosen = lane_of // 48 == row_of % 16
    both = jnp.concatenate(
        [jnp.broadcast_to(coarse.astype(F32), (16, 128)), jnp.broadcast_to(fine.astype(F32), (16, 128))], 0
    ).astype(BF16)
    for patch in range(2):
        coefficients = jnp.where(
            chosen, jnp.dot(both, spread[patch], preferred_element_type=F32), 0.0
        ).astype(BF16)
        kernel_power = powers[patch]

        def finish(number, carry):
            rows = pl.ds(pl.multiple_of(number * 16, 16), 16)
            product = jnp.dot(coefficients, conv[rows].reshape(768, 256), preferred_element_type=F32)
            model = product[0:16] + product[16:32]
            mask = coverage[rows].astype(F32)
            difference[rows] = mask * (science[rows] - model)
            variance[rows] = mask * (science_var[rows] + kernel_power * template_var[rows])
            return carry

        lax.fori_loop(16 * patch, 16 * patch + 16, finish, 0)

    each_sent(halo, lambda copy: copy.wait_send())
    each_sent(gram_copy, lambda copy: copy.wait_send())


def local(template, template_var, coverage, exposure, exposure_var, strip_owner, strip_slot):
    def blocks(array):
        return array.reshape(128, 4, 2, 128).transpose(0, 2, 1, 3).reshape(128, 8, 128)

    vmem = pl.BlockSpec(memory_space=pltpu.VMEM)
    dma = pltpu.SemaphoreType.DMA
    return pl.pallas_call(
        kernel,
        out_shape=[jax.ShapeDtypeStruct((512, 256), F32)] * 2,
        in_specs=[vmem] * 11,
        out_specs=[vmem] * 2,
        scratch_shapes=[
            pltpu.VMEM((544, 512), BF16),
            pltpu.VMEM((16, 608, 256), BF16),
            pltpu.VMEM((512, 48, 256), BF16),
            pltpu.VMEM((128, 16, 128), BF16),
            pltpu.VMEM((128, 16, 128), BF16),
            pltpu.VMEM((128, 128), jnp.int32),
            pltpu.VMEM((512, 256), F32),
            pltpu.VMEM((512, 256), F32),
            pltpu.VMEM((512, 256), F32),
            pltpu.VMEM((48, 128), F32),
            pltpu.VMEM((8, 48, 128), F32),
            pltpu.VMEM((8, 128), jnp.int32),
            pltpu.SMEM((8, 128), jnp.int32),
            pltpu.SMEM((8, 128), jnp.int32),
            dma((8,)), dma((8,)), dma, dma, dma((2,)), dma((2,)), dma((8,)), dma((8,)),
        ],
        compiler_params=pltpu.CompilerParams(
            collective_id=0, has_side_effects=True, vmem_limit_bytes=60 * 1024 * 1024
        ),
        cost_estimate=pl.CostEstimate(flops=10**10, bytes_accessed=8 * 10**6, transcendentals=0),
    )(
        template, template_var, coverage, blocks(exposure), blocks(exposure_var), strip_owner, strip_slot,
        *[jnp.asarray(table) for table in tables()],
    )


def solution(mesh):
    image = P("row", "col")
    strips = P("row", "col", None, None)
    return jax.shard_map(
        local,
        mesh=mesh,
        in_specs=(image, image, image, strips, strips, image, image),
        out_specs=(image, image),
        check_vma=False,
    )
```

profile of v0, /device:TPU:12, one launch (start us, length us, event | category | flops | bytes accessed | tf_op | source)
XLA Modules:
  0.0 63.2 jit_solution(14788930782292836435)
XLA Ops:
  0.6 58.8 %shard_map.122 = (f32[512,256]{1,0:T(8,128)}, f32[512,256]{1,0:T(8,128)}) custom-call(f32[512,256]{1,0:T(8,128)} %template.1, f32[512,256]{1,0:T(8,128)} %template_var.1, s32[512,256]{1,0:T(8,128)} %coverage.1, f32[128,8,128]{2,1,0:T(8,128)} %bitcast.10, f32[128,8,128]{2,1,0:T(8,128)} %bitcast.11, s32[1,128]{1,0:T(1,128)} %owner.1, s32[1,128]{1,0:T(1,128)} %slot.1, ...), custom_call_target="tpu_custom_call" | custom-call | flops 10000000000 | bytes 8000000 | tf_op jit(solution)/shard_map/pallas_call | solution.py:365
  59.4 1.9 %copy.17 = f32[512,256]{1,0:T(8,128)} copy(f32[512,256]{1,0:T(8,128)} %get-tuple-element.4) | data formatting | bytes 1048576
  61.3 1.9 %copy.18 = f32[512,256]{1,0:T(8,128)} copy(f32[512,256]{1,0:T(8,128)} %get-tuple-element.5) | data formatting | bytes 1048576
where the time goes:
time: 63.4 us; the launch traced here: 63.2 us
  Pallas kernels  58.8 us (93%)
  local copies, waits for them, and re-layouts  3.74 us (6%)
  between operations  0.64 us (1%)
    pallas_call x1, Pallas kernels, local(): pl.pallas_call(kernel, out_shape=[jax.ShapeDtypeStruct((512, 256), F32)]...  58.8 us
    unnamed x2, local copies, waits for them, and re-layouts  3.74 us

commit v1 on v0

--- a/solution.py
+++ b/solution.py
@@ -216,7 +216,7 @@
                 ]
         return carry
 
-    lax.fori_loop(0, 8, along_x, 0)
+    lax.fori_loop(0, 8, along_x, 0, unroll=True)
 
     def label_wait(count, which):
         part = labels.at[pl.ds(0, count)]
@@ -250,7 +250,7 @@
         along_y(pl.multiple_of(number * BLOCK, 16), BLOCK)
         return carry
 
-    lax.fori_loop(0, 5, y_block, 0)
+    lax.fori_loop(0, 5, y_block, 0, unroll=True)
     along_y(480, 32)
 
     label_wait(112, 1)
@@ -276,9 +276,9 @@
     is_target = lax.broadcasted_iota(jnp.int32, (16, 256), 0) == TARGET - 32
 
     def gram_rows(number, total):
-        base = pl.multiple_of(number * 8, 8)
+        base = pl.multiple_of(number * 64, 64)
         pieces = []
-        for row in range(8):
+        for row in range(64):
             weight = root[pl.ds(base + row, 1), :]
             goal = weight * science[pl.ds(base + row, 1), :]
             basis = conv[base + row].astype(F32) * weight
@@ -291,7 +291,7 @@
 
     own_gram[...] = jnp.zeros_like(own_gram)
     for patch in range(2):
-        total = lax.fori_loop(32 * patch, 32 * patch + 32, gram_rows, jnp.zeros((48, 48), F32))
+        total = lax.fori_loop(4 * patch, 4 * patch + 4, gram_rows, jnp.zeros((48, 48), F32))
         own_gram[:, patch * 64 : patch * 64 + 48] = total
 
     each_sent(gram_copy, lambda copy: copy.start())
@@ -312,15 +312,12 @@
     ridge = jnp.where(lane < 64, trace_upper, trace_lower) * (RIDGE / 45.0)
     system = jnp.where(diagonal, system + ridge, system)
 
-    def eliminate(step, system):
-        pivot_row = jnp.sum(jnp.where(sub == step, system, 0.0), 0, keepdims=True)
-        pick = (lane - half_lane) + step
-        column = jnp.take_along_axis(system, pick, axis=1)
-        pivot = jnp.sum(jnp.where(sub == step, column, 0.0), 0, keepdims=True)
-        scaled = column * (1.0 / pivot)
-        return jnp.where(half_lane == step, scaled, system - scaled * pivot_row)
-
-    system = lax.fori_loop(0, 45, eliminate, system)
+    for step in range(45):
+        column = jnp.take_along_axis(system, (lane - half_lane) + step, axis=1)
+        inverse = 1.0 / column[step : step + 1]
+        system = jnp.where(
+            half_lane == step, column * inverse, system - column * (inverse * system[step : step + 1])
+        )
     answer = jnp.where(jnp.logical_and(half_lane[47:48] < 45, lane[47:48] < 128), system[TARGET : TARGET + 1], 0.0)
     terms = power[...] * answer
     upper_terms = jnp.sum(jnp.where(lane < 64, terms, 0.0), 1, keepdims=True)
@@ -350,7 +347,7 @@
             variance[rows] = mask * (science_var[rows] + kernel_power * template_var[rows])
             return carry
 
-        lax.fori_loop(16 * patch, 16 * patch + 16, finish, 0)
+        lax.fori_loop(16 * patch, 16 * patch + 16, finish, 0, unroll=8)
 
     each_sent(halo, lambda copy: copy.wait_send())
     each_sent(gram_copy, lambda copy: copy.wait_send())

time: 63.4 us -> 48.1 us (0.76)
  Pallas kernels: 58.8 us -> 43.5 us
    pallas_call x1, Pallas kernels: 58.8 us -> 43.5 us  [local(): pl.pallas_call(kernel, out_shape=[jax.ShapeDtypeStruct((512, 256), F32)]...]
where the time goes in v1:
time: 48.1 us; the launch traced here: 47.9 us
  Pallas kernels  43.5 us (90%)
  local copies, waits for them, and re-layouts  3.74 us (8%)
  between operations  0.64 us (1%)
    pallas_call x1, Pallas kernels, local(): pl.pallas_call(kernel, out_shape=[jax.ShapeDtypeStruct((512, 256), F32)]...  43.5 us
    unnamed x2, local copies, waits for them, and re-layouts  3.74 us

profile of v1, /device:TPU:12, one launch (start us, length us, event | category | flops | bytes accessed | tf_op | source)
XLA Modules:
  0.0 47.9 jit_solution(17907366992838104412)
XLA Ops:
  0.6 43.5 %shard_map.122 = (f32[512,256]{1,0:T(8,128)}, f32[512,256]{1,0:T(8,128)}) custom-call(f32[512,256]{1,0:T(8,128)} %template.1, f32[512,256]{1,0:T(8,128)} %template_var.1, s32[512,256]{1,0:T(8,128)} %coverage.1, f32[128,8,128]{2,1,0:T(8,128)} %bitcast.10, f32[128,8,128]{2,1,0:T(8,128)} %bitcast.11, s32[1,128]{1,0:T(1,128)} %owner.1, s32[1,128]{1,0:T(1,128)} %slot.1, ...), custom_call_target="tpu_custom_call" | custom-call | flops 10000000000 | bytes 8000000 | tf_op jit(solution)/shard_map/pallas_call | solution.py:362
  44.1 1.9 %copy.17 = f32[512,256]{1,0:T(8,128)} copy(f32[512,256]{1,0:T(8,128)} %get-tuple-element.4) | data formatting | bytes 1048576
  46.0 1.9 %copy.18 = f32[512,256]{1,0:T(8,128)} copy(f32[512,256]{1,0:T(8,128)} %get-tuple-element.5) | data formatting | bytes 1048576

commit v2 on v1

--- a/solution.py
+++ b/solution.py
@@ -85,11 +85,13 @@
 
 
 def kernel(
-    template, template_var, coverage, flux, noise, owner, slot, x_weights, y_weights, power, spread,
-    difference, variance,
+    template_hbm, template_var_hbm, coverage_hbm, flux_hbm, noise_hbm, x_weights_hbm, y_weights_hbm, spread_hbm,
+    owner, slot, power,
+    residual_hbm, spread_var_hbm,
+    template, template_var, coverage, flux, noise, x_weights, y_weights, spread, residual, spread_var,
     wide, filtered, conv, send, recv, labels, science, science_var, root, own_gram, near_gram,
     row_index, table_in, table_out,
-    halo_out, halo_in, part_out, part_in, label_out, label_in, gram_out, gram_in,
+    halo_out, halo_in, part_out, part_in, label_out, label_in, gram_out, gram_in, load_in, store_out,
 ):
     r = lax.axis_index("row")
     c = lax.axis_index("col")
@@ -98,6 +100,16 @@
     place = (z * 2 + k) * 16 + r * 4 + x
     barrier = pltpu.get_barrier_semaphore()
 
+    loads = [
+        pltpu.make_async_copy(source, held, load_in.at[number])
+        for number, (source, held) in enumerate((
+            (flux_hbm, flux), (noise_hbm, noise), (template_hbm, template), (x_weights_hbm, x_weights),
+            (y_weights_hbm, y_weights), (coverage_hbm, coverage), (template_var_hbm, template_var), (spread_hbm, spread),
+        ))
+    ]
+    for load in loads:
+        load.start()
+
     wide[...] = jnp.zeros_like(wide)
     near_gram[...] = jnp.zeros_like(near_gram)
 
@@ -108,11 +120,14 @@
 
     lax.fori_loop(1, 128, greet, 0)
 
+    labels[pl.ds(place, 1), :] = slot[...]
+    owners = jnp.transpose(jnp.broadcast_to(owner[...], (128, 128)))
+    row_index[...] = jnp.broadcast_to(inverse_row(owners), (8, 128))
+    pltpu.sync_copy(row_index, table_in)
+    loads[2].wait()
     wide[16:528, 128:384] = template[...].astype(BF16)
-    labels[pl.ds(place, 1), :] = slot[...]
-    columns = jnp.transpose(jnp.broadcast_to(owner[...], (128, 128)))
-    row_index[...] = jnp.broadcast_to(inverse_row(columns), (8, 128))
-    pltpu.sync_copy(row_index, table_in)
+    loads[0].wait()
+    loads[1].wait()
 
     def pack(number, carry):
         block = within(table_in[0, number])
@@ -204,6 +219,7 @@
 
     each_received(halo)
 
+    loads[3].wait()
     whole = wide[...]
     windows = (whole[:, 64:320], whole[:, 192:448])
 
@@ -246,6 +262,8 @@
                 groups.append(total.reshape(rows, 8, 256))
             conv[pl.ds(first, rows), pair * 16 : pair * 16 + 16, :] = jnp.concatenate(groups, 1).astype(BF16)
 
+    loads[4].wait()
+
     def y_block(number, carry):
         along_y(pl.multiple_of(number * BLOCK, 16), BLOCK)
         return carry
@@ -271,6 +289,7 @@
         return carry
 
     lax.fori_loop(0, 64, unpack, 0, unroll=4)
+    loads[5].wait()
     root[...] = coverage[...].astype(F32) * lax.rsqrt(science_var[...])
 
     is_target = lax.broadcasted_iota(jnp.int32, (16, 256), 0) == TARGET - 32
@@ -312,12 +331,33 @@
     ridge = jnp.where(lane < 64, trace_upper, trace_lower) * (RIDGE / 45.0)
     system = jnp.where(diagonal, system + ridge, system)
 
-    for step in range(45):
-        column = jnp.take_along_axis(system, (lane - half_lane) + step, axis=1)
-        inverse = 1.0 / column[step : step + 1]
-        system = jnp.where(
-            half_lane == step, column * inverse, system - column * (inverse * system[step : step + 1])
-        )
+    def column_of(matrix, step):
+        return jnp.take_along_axis(matrix, (lane - half_lane) + step, axis=1)
+
+    def pivot_pair(first, second, step):
+        a, b = first[step : step + 1], second[step : step + 1]
+        c, d = first[step + 1 : step + 2], second[step + 1 : step + 2]
+        inverse = 1.0 / (a * d - b * c)
+        return first * (d * inverse) - second * (c * inverse), second * (a * inverse) - first * (b * inverse)
+
+    for step in range(0, 44, 4):
+        columns = [column_of(system, step + number) for number in range(4)]
+        row = [system[step + number : step + number + 1] for number in range(4)]
+        u0, u1 = pivot_pair(columns[0], columns[1], step)
+        third, fourth = (
+            column - u0 * column[step : step + 1] - u1 * column[step + 1 : step + 2] for column in columns[2:]
+        )
+        u2, u3 = pivot_pair(third, fourth, step + 2)
+        row[2] = row[2] - u0[step + 2 : step + 3] * row[0] - u1[step + 2 : step + 3] * row[1]
+        row[3] = row[3] - u0[step + 3 : step + 4] * row[0] - u1[step + 3 : step + 4] * row[1]
+        v0 = u0 - u2 * u0[step + 2 : step + 3] - u3 * u0[step + 3 : step + 4]
+        v1 = u1 - u2 * u1[step + 2 : step + 3] - u3 * u1[step + 3 : step + 4]
+        system = system - u0 * row[0] - u1 * row[1] - u2 * row[2] - u3 * row[3]
+        for number, column in enumerate((v0, v1, u2, u3)):
+            system = jnp.where(half_lane == step + number, column, system)
+    column = column_of(system, 44)
+    inverse = 1.0 / column[44:45]
+    system = jnp.where(half_lane == 44, column * inverse, system - column * (inverse * system[44:45]))
     answer = jnp.where(jnp.logical_and(half_lane[47:48] < 45, lane[47:48] < 128), system[TARGET : TARGET + 1], 0.0)
     terms = power[...] * answer
     upper_terms = jnp.sum(jnp.where(lane < 64, terms, 0.0), 1, keepdims=True)
@@ -332,6 +372,9 @@
     both = jnp.concatenate(
         [jnp.broadcast_to(coarse.astype(F32), (16, 128)), jnp.broadcast_to(fine.astype(F32), (16, 128))], 0
     ).astype(BF16)
+    loads[6].wait()
+    loads[7].wait()
+    stores = []
     for patch in range(2):
         coefficients = jnp.where(
             chosen, jnp.dot(both, spread[patch], preferred_element_type=F32), 0.0
@@ -342,15 +385,21 @@
             rows = pl.ds(pl.multiple_of(number * 16, 16), 16)
             product = jnp.dot(coefficients, conv[rows].reshape(768, 256), preferred_element_type=F32)
             model = product[0:16] + product[16:32]
-            mask = coverage[rows].astype(F32)
-            difference[rows] = mask * (science[rows] - model)
-            variance[rows] = mask * (science_var[rows] + kernel_power * template_var[rows])
+            residual[rows] = science[rows] - model
+            spread_var[rows] = science_var[rows] + kernel_power * template_var[rows]
             return carry
 
         lax.fori_loop(16 * patch, 16 * patch + 16, finish, 0, unroll=8)
+        part = pl.ds(256 * patch, 256)
+        for number, (held, goal) in enumerate(((residual, residual_hbm), (spread_var, spread_var_hbm))):
+            store = pltpu.make_async_copy(held.at[part], goal.at[part], store_out.at[2 * patch + number])
+            store.start()
+            stores.append(store)
 
     each_sent(halo, lambda copy: copy.wait_send())
     each_sent(gram_copy, lambda copy: copy.wait_send())
+    for store in stores:
+        store.wait()
 
 
 def local(template, template_var, coverage, exposure, exposure_var, strip_owner, strip_slot):
@@ -358,13 +407,25 @@
         return array.reshape(128, 4, 2, 128).transpose(0, 2, 1, 3).reshape(128, 8, 128)
 
     vmem = pl.BlockSpec(memory_space=pltpu.VMEM)
+    hbm = pl.BlockSpec(memory_space=pltpu.HBM)
     dma = pltpu.SemaphoreType.DMA
-    return pl.pallas_call(
+    x_weights, y_weights, power, spread = [jnp.asarray(table) for table in tables()]
+    residual, spread_var = pl.pallas_call(
         kernel,
         out_shape=[jax.ShapeDtypeStruct((512, 256), F32)] * 2,
-        in_specs=[vmem] * 11,
-        out_specs=[vmem] * 2,
+        in_specs=[hbm] * 8 + [vmem] * 3,
+        out_specs=[hbm] * 2,
         scratch_shapes=[
+            pltpu.VMEM((512, 256), F32),
+            pltpu.VMEM((512, 256), F32),
+            pltpu.VMEM((512, 256), jnp.int32),
+            pltpu.VMEM((128, 8, 128), F32),
+            pltpu.VMEM((128, 8, 128), F32),
+            pltpu.VMEM((8, 256, 256), BF16),
+            pltpu.VMEM((8, BLOCK * 8, 256), BF16),
+            pltpu.VMEM((2, 128, 768), BF16),
+            pltpu.VMEM((512, 256), F32),
+            pltpu.VMEM((512, 256), F32),
             pltpu.VMEM((544, 512), BF16),
             pltpu.VMEM((16, 608, 256), BF16),
             pltpu.VMEM((512, 48, 256), BF16),
@@ -379,16 +440,18 @@
             pltpu.VMEM((8, 128), jnp.int32),
             pltpu.SMEM((8, 128), jnp.int32),
             pltpu.SMEM((8, 128), jnp.int32),
-            dma((8,)), dma((8,)), dma, dma, dma((2,)), dma((2,)), dma((8,)), dma((8,)),
+            dma((8,)), dma((8,)), dma, dma, dma((2,)), dma((2,)), dma((8,)), dma((8,)), dma((8,)), dma((4,)),
         ],
         compiler_params=pltpu.CompilerParams(
             collective_id=0, has_side_effects=True, vmem_limit_bytes=60 * 1024 * 1024
         ),
         cost_estimate=pl.CostEstimate(flops=10**10, bytes_accessed=8 * 10**6, transcendentals=0),
     )(
-        template, template_var, coverage, blocks(exposure), blocks(exposure_var), strip_owner, strip_slot,
-        *[jnp.asarray(table) for table in tables()],
+        template, template_var, coverage, blocks(exposure), blocks(exposure_var), x_weights, y_weights, spread,
+        strip_owner, strip_slot, power,
     )
+    mask = coverage.astype(F32)
+    return (mask * residual, mask * spread_var)
 
 
 def solution(mesh):

time: 48.1 us -> 42.2 us (0.88)
  Pallas kernels: 43.5 us -> 39.1 us
  local copies, waits for them, and re-layouts: 3.74 us -> 0.01 us
  other arithmetic: 0 us -> 2.27 us
    pallas_call x1, Pallas kernels: 43.5 us -> 39.1 us  [local(): pl.pallas_call(kernel, out_shape=[jax.ShapeDtypeStruct((512, 256), F32)]...]
    unnamed x2, local copies, waits for them, and re-layouts: 3.74 us -> 0.01 us
    mul x0 -> x1, other arithmetic: none -> 2.27 us  [local(): return (mask * residual, mask * spread_var)]
where the time goes in v2:
time: 42.2 us; the launch traced here: 42 us
  Pallas kernels  39.1 us (93%)
  other arithmetic  2.27 us (5%)
  between operations  0.66 us (2%)
    pallas_call x1, Pallas kernels, local(): pl.pallas_call(kernel, out_shape=[jax.ShapeDtypeStruct((512, 256), F32)]...  39.1 us
    mul x1, other arithmetic, local(): return (mask * residual, mask * spread_var)  2.27 us

profile of v2, /device:TPU:12, one launch (start us, length us, event | category | flops | bytes accessed | tf_op | source)
XLA Modules:
  0.0 42.0 jit_solution(6944991089452000838)
XLA Ops:
  0.6 0.0 copy-start
  0.6 39.1 %shard_map.122 = (f32[512,256]{1,0:T(8,128)}, f32[512,256]{1,0:T(8,128)}) custom-call(f32[512,256]{1,0:T(8,128)} %template_hbm.1, f32[512,256]{1,0:T(8,128)} %template_var_hbm.1, s32[512,256]{1,0:T(8,128)} %coverage_hbm.1, f32[128,8,128]{2,1,0:T(8,128)} %bitcast.10, f32[128,8,128]{2,1,0:T(8,128)} %bitcast.11, ...), custom_call_target="tpu_custom_call" | custom-call | flops 10000000000 | bytes 8000000 | tf_op jit(solution)/shard_map/pallas_call | solution.py:413
  39.7 0.0 copy-done
  39.7 2.3 %convert_multiply_fusion = (f32[512,256]{1,0:T(8,128)}, f32[512,256]{1,0:T(8,128)}) fusion(f32[512,256]{1,0:T(8,128)} %get-tuple-element.5, s32[512,256]{1,0:T(8,128)S(1)} %copy-done, f32[512,256]{1,0:T(8,128)} %get-tuple-element.4), kind=kLoop, calls=%fused_computation | loop fusion | flops 393216 | bytes 2621440 | tf_op jit(solution)/shard_map/mul | solution.py:454
Async XLA Ops:
  0.6 39.1 %copy-start = (s32[512,256]{1,0:T(8,128)S(1)}, s32[512,256]{1,0:T(8,128)}, u32[]{:S(2)}) copy-start(s32[512,256]{1,0:T(8,128)} %coverage_hbm.1) | copy-start | bytes 1572868

commit v3 on v2

--- a/solution.py
+++ b/solution.py
@@ -19,6 +19,7 @@
 GROUP_OF_PASS = (0, 1, 2, 3, 4, 4, 5, 5)
 BLOCK = 96
 TARGET = 47
+GRAM_COPIES = ((0, -1, 0), (1, 1, 0), (0, -1, -1), (0, -1, 1), (1, 1, -1), (1, 1, 1), (0, 0, -1), (0, 0, 1), (1, 0, -1), (1, 0, 1))
 DIRECTIONS = ((0, -1), (0, 1), (-1, 0), (1, 0), (-1, -1), (-1, 1), (1, -1), (1, 1))
 
 
@@ -87,11 +88,11 @@
 def kernel(
     template_hbm, template_var_hbm, coverage_hbm, flux_hbm, noise_hbm, x_weights_hbm, y_weights_hbm, spread_hbm,
     owner, slot, power,
-    residual_hbm, spread_var_hbm,
-    template, template_var, coverage, flux, noise, x_weights, y_weights, spread, residual, spread_var,
+    residual, spread_var,
+    template, template_var, coverage, flux, noise, x_weights, y_weights, spread,
     wide, filtered, conv, send, recv, labels, science, science_var, root, own_gram, near_gram,
     row_index, table_in, table_out,
-    halo_out, halo_in, part_out, part_in, label_out, label_in, gram_out, gram_in, load_in, store_out,
+    halo_out, halo_in, part_out, part_in, label_out, label_in, gram_out, gram_in, load_in, ready,
 ):
     r = lax.axis_index("row")
     c = lax.axis_index("col")
@@ -103,7 +104,7 @@
     loads = [
         pltpu.make_async_copy(source, held, load_in.at[number])
         for number, (source, held) in enumerate((
-            (flux_hbm, flux), (noise_hbm, noise), (template_hbm, template), (x_weights_hbm, x_weights),
+            (template_hbm, template), (flux_hbm, flux), (noise_hbm, noise), (x_weights_hbm, x_weights),
             (y_weights_hbm, y_weights), (coverage_hbm, coverage), (template_var_hbm, template_var), (spread_hbm, spread),
         ))
     ]
@@ -112,32 +113,21 @@
 
     wide[...] = jnp.zeros_like(wide)
     near_gram[...] = jnp.zeros_like(near_gram)
-
-    def greet(step, carry):
-        other = lax.rem(me + step, 128)
-        pl.semaphore_signal(barrier, inc=1, device_id=(other // 32, other % 32), device_id_type=MESH)
-        return carry
-
-    lax.fori_loop(1, 128, greet, 0)
+    own_gram[...] = jnp.zeros_like(own_gram)
+
+    def column(dx, dz, dk):
+        return (x + dx) % 4 * 8 + (z + dz) % 4 * 2 + (k + dk) % 2
+
+    across = [((r + dr) % 4, column(dx, 0, 0)) for dr in range(4) for dx in range(4) if dr or dx]
+    along = [(r, column(0, dz, dk)) for dz in range(4) for dk in range(2) if dz or dk]
+    around = [((r + dr) % 4, (c + dc) % 32) for dr, dc in DIRECTIONS]
+    for other in around + across + along:
+        pl.semaphore_signal(barrier, inc=1, device_id=other, device_id_type=MESH)
 
     labels[pl.ds(place, 1), :] = slot[...]
-    owners = jnp.transpose(jnp.broadcast_to(owner[...], (128, 128)))
-    row_index[...] = jnp.broadcast_to(inverse_row(owners), (8, 128))
-    pltpu.sync_copy(row_index, table_in)
-    loads[2].wait()
+    loads[0].wait()
     wide[16:528, 128:384] = template[...].astype(BF16)
-    loads[0].wait()
-    loads[1].wait()
-
-    def pack(number, carry):
-        block = within(table_in[0, number])
-        send[number] = jnp.concatenate([flux[block], noise[block]], 0).astype(BF16)
-        return carry
-
-    lax.fori_loop(0, 128, pack, 0, unroll=4)
-    recv[place] = send[me]
-    filtered[:, 544:608, :] = jnp.zeros((16, 64, 256), BF16)
-    pl.semaphore_wait(barrier, 127)
+    pl.semaphore_wait(barrier, 30)
 
     def inside(dr, dc):
         return jnp.logical_and(
@@ -164,15 +154,27 @@
         )
 
     def gram_copy(number):
-        dr, dc = DIRECTIONS[number]
+        patch, dr, dc = GRAM_COPIES[number]
         return pltpu.make_async_remote_copy(
-            src_ref=own_gram,
+            src_ref=own_gram.at[patch],
             dst_ref=near_gram.at[number],
             send_sem=gram_out.at[number],
             recv_sem=gram_in.at[number],
             device_id=target(dr, dc),
             device_id_type=MESH,
         )
+
+    def grams_sent(action):
+        for number, (_, dr, dc) in enumerate(GRAM_COPIES):
+            @pl.when(inside(dr, dc))
+            def _():
+                action(gram_copy(number))
+
+    def grams_received():
+        for number, (_, dr, dc) in enumerate(GRAM_COPIES):
+            @pl.when(inside(-dr, -dc))
+            def _():
+                gram_copy(number).wait_recv()
 
     def each_sent(make, action):
         for number, (dr, dc) in enumerate(DIRECTIONS):
@@ -198,10 +200,25 @@
             device_id_type=MESH,
         )
 
-    for dr in range(4):
-        for dx in range(4):
-            if dr or dx:
-                label_copy(place, 1, (r + dr) % 4, ((x + dx) % 4) * 8 + z * 2 + k, 0).start()
+    for other in along:
+        pl.semaphore_signal(ready, inc=1, device_id=other, device_id_type=MESH)
+    for other in across:
+        label_copy(place, 1, *other, 0).start()
+
+    owners = jnp.transpose(jnp.broadcast_to(owner[...], (128, 128)))
+    row_index[...] = jnp.broadcast_to(inverse_row(owners), (8, 128))
+    pltpu.sync_copy(row_index, table_in)
+    loads[1].wait()
+    loads[2].wait()
+
+    def pack(number, carry):
+        block = within(table_in[0, number])
+        send[number] = jnp.concatenate([flux[block], noise[block]], 0).astype(BF16)
+        return carry
+
+    lax.fori_loop(0, 128, pack, 0, unroll=4)
+    recv[place] = send[me]
+    pl.semaphore_wait(ready, 7)
 
     def send_part(step, carry):
         other = lax.rem(me + step, 128)
@@ -219,6 +236,7 @@
 
     each_received(halo)
 
+    filtered[:, 544:608, :] = jnp.zeros((16, 64, 256), BF16)
     loads[3].wait()
     whole = wide[...]
     windows = (whole[:, 64:320], whole[:, 192:448])
@@ -240,12 +258,8 @@
         pltpu.make_async_copy(part, part, label_out.at[which]).wait()
 
     label_wait(15, 0)
-    for dz in range(4):
-        for dk in range(2):
-            if dz or dk:
-                label_copy(
-                    pl.multiple_of((z * 2 + k) * 16, 16), 16, r, x * 8 + ((z + dz) % 4) * 2 + (k + dk) % 2, 1
-                ).start()
+    for other in along:
+        label_copy(pl.multiple_of((z * 2 + k) * 16, 16), 16, *other, 1).start()
 
     def along_y(first, rows):
         for pair in range(3):
@@ -294,35 +308,38 @@
 
     is_target = lax.broadcasted_iota(jnp.int32, (16, 256), 0) == TARGET - 32
 
-    def gram_rows(number, total):
-        base = pl.multiple_of(number * 64, 64)
+    def gram_patch(patch, carry):
+        base = pl.multiple_of(patch * 256, 256)
         pieces = []
-        for row in range(64):
+        for row in range(256):
             weight = root[pl.ds(base + row, 1), :]
             goal = weight * science[pl.ds(base + row, 1), :]
             basis = conv[base + row].astype(F32) * weight
             last = jnp.where(is_target, goal, basis[32:48])
             pieces.append(jnp.concatenate([basis[0:32].astype(BF16), last.astype(BF16)], 0))
         block = jnp.concatenate(pieces, 1)
-        return total + lax.dot_general(
-            block, block, (((1,), (1,)), ((), ())), preferred_element_type=F32
-        )
-
-    own_gram[...] = jnp.zeros_like(own_gram)
-    for patch in range(2):
-        total = lax.fori_loop(4 * patch, 4 * patch + 4, gram_rows, jnp.zeros((48, 48), F32))
-        own_gram[:, patch * 64 : patch * 64 + 48] = total
-
-    each_sent(gram_copy, lambda copy: copy.start())
-    each_received(gram_copy)
+        total = lax.dot_general(block, block, (((1,), (1,)), ((), ())), preferred_element_type=F32)
+        own_gram[patch, :, 0:48] = total[0:24]
+        own_gram[patch, :, 64:112] = total[24:48]
+        return carry
+
+    lax.fori_loop(0, 2, gram_patch, 0)
+    grams_sent(lambda copy: copy.start())
+    grams_received()
 
     lane = lax.broadcasted_iota(jnp.int32, (48, 128), 1)
     sub = lax.broadcasted_iota(jnp.int32, (48, 128), 0)
-    beside = own_gram[...] + near_gram[0] + near_gram[1]
-    from_below = near_gram[2] + near_gram[4] + near_gram[5]
-    from_above = near_gram[3] + near_gram[6] + near_gram[7]
-    moved = beside + jnp.where(lane < 64, from_below, from_above)
-    system = beside + pltpu.roll(moved, 64, 1)
+    beside = own_gram[0] + own_gram[1] + near_gram[6] + near_gram[7] + near_gram[8] + near_gram[9]
+    upper = beside + near_gram[1] + near_gram[4] + near_gram[5]
+    lower = beside + near_gram[0] + near_gram[2] + near_gram[3]
+    first_half = lane[0:24] < 64
+    system = jnp.concatenate(
+        [
+            jnp.where(first_half, upper, pltpu.roll(lower, 64, 1)),
+            jnp.where(first_half, pltpu.roll(upper, 64, 1), lower),
+        ],
+        0,
+    )
     half_lane = lane % 64
     diagonal = jnp.logical_and(sub == half_lane, sub < 45)
     on_diagonal = jnp.where(diagonal, system, 0.0)
@@ -374,7 +391,6 @@
     ).astype(BF16)
     loads[6].wait()
     loads[7].wait()
-    stores = []
     for patch in range(2):
         coefficients = jnp.where(
             chosen, jnp.dot(both, spread[patch], preferred_element_type=F32), 0.0
@@ -390,16 +406,9 @@
             return carry
 
         lax.fori_loop(16 * patch, 16 * patch + 16, finish, 0, unroll=8)
-        part = pl.ds(256 * patch, 256)
-        for number, (held, goal) in enumerate(((residual, residual_hbm), (spread_var, spread_var_hbm))):
-            store = pltpu.make_async_copy(held.at[part], goal.at[part], store_out.at[2 * patch + number])
-            store.start()
-            stores.append(store)
 
     each_sent(halo, lambda copy: copy.wait_send())
-    each_sent(gram_copy, lambda copy: copy.wait_send())
-    for store in stores:
-        store.wait()
+    grams_sent(lambda copy: copy.wait_send())
 
 
 def local(template, template_var, coverage, exposure, exposure_var, strip_owner, strip_slot):
@@ -412,9 +421,9 @@
     x_weights, y_weights, power, spread = [jnp.asarray(table) for table in tables()]
     residual, spread_var = pl.pallas_call(
         kernel,
-        out_shape=[jax.ShapeDtypeStruct((512, 256), F32)] * 2,
+        out_shape=[pltpu.VMEM((512, 256), F32)] * 2,
         in_specs=[hbm] * 8 + [vmem] * 3,
-        out_specs=[hbm] * 2,
+        out_specs=[vmem] * 2,
         scratch_shapes=[
             pltpu.VMEM((512, 256), F32),
             pltpu.VMEM((512, 256), F32),
@@ -424,8 +433,6 @@
             pltpu.VMEM((8, 256, 256), BF16),
             pltpu.VMEM((8, BLOCK * 8, 256), BF16),
             pltpu.VMEM((2, 128, 768), BF16),
-            pltpu.VMEM((512, 256), F32),
-            pltpu.VMEM((512, 256), F32),
             pltpu.VMEM((544, 512), BF16),
             pltpu.VMEM((16, 608, 256), BF16),
             pltpu.VMEM((512, 48, 256), BF16),
@@ -435,12 +442,12 @@
             pltpu.VMEM((512, 256), F32),
             pltpu.VMEM((512, 256), F32),
             pltpu.VMEM((512, 256), F32),
-            pltpu.VMEM((48, 128), F32),
-            pltpu.VMEM((8, 48, 128), F32),
+            pltpu.VMEM((2, 24, 128), F32),
+            pltpu.VMEM((10, 24, 128), F32),
             pltpu.VMEM((8, 128), jnp.int32),
             pltpu.SMEM((8, 128), jnp.int32),
             pltpu.SMEM((8, 128), jnp.int32),
-            dma((8,)), dma((8,)), dma, dma, dma((2,)), dma((2,)), dma((8,)), dma((8,)), dma((8,)), dma((4,)),
+            dma((8,)), dma((8,)), dma, dma, dma((2,)), dma((2,)), dma((10,)), dma((10,)), dma((8,)), pltpu.SemaphoreType.REGULAR,
         ],
         compiler_params=pltpu.CompilerParams(
             collective_id=0, has_side_effects=True, vmem_limit_bytes=60 * 1024 * 1024

time: 42.2 us -> 36.9 us (0.87)
  the two profiles are of different devices: /device:TPU:12 before, /device:TPU:1 now
where the time goes in v3:
time: 36.9 us; the launch traced here: 36.5 us
  Pallas kernels  34.7 us (94%)
  other arithmetic  1.07 us (3%)
  between operations  0.66 us (2%)
    pallas_call x1, Pallas kernels, local(): pl.pallas_call(kernel, out_shape=[pltpu.VMEM((512, 256), F32)] * 2, in_sp...  34.7 us
    mul x1, other arithmetic, local(): return (mask * residual, mask * spread_var)  1.07 us

profile of v3, /device:TPU:1, one launch (start us, length us, event | category | flops | bytes accessed | tf_op | source)
XLA Modules:
  0.0 36.5 jit_solution(1297993218567075098)
XLA Ops:
  0.6 0.0 copy-start
  0.6 34.7 %shard_map.122 = (f32[512,256]{1,0:T(8,128)S(1)}, f32[512,256]{1,0:T(8,128)S(1)}) custom-call(f32[512,256]{1,0:T(8,128)} %template_hbm.1, f32[512,256]{1,0:T(8,128)} %template_var_hbm.1, s32[512,256]{1,0:T(8,128)} %coverage_hbm.1, f32[128,8,128]{2,1,0:T(8,128)} %bitcast.10, f32[128,8,128]{2,1,0:T(8,128)} %bitcast.11, ...), custom_call_target="tpu_custom_call" | custom-call | flops 10000000000 | bytes 8000000 | tf_op jit(solution)/shard_map/pallas_call | solution.py:422
  35.4 0.0 copy-done
  35.4 1.1 %convert_multiply_fusion = (f32[512,256]{1,0:T(8,128)}, f32[512,256]{1,0:T(8,128)}) fusion(f32[512,256]{1,0:T(8,128)S(1)} %get-tuple-element.5, s32[512,256]{1,0:T(8,128)S(1)} %copy-done, f32[512,256]{1,0:T(8,128)S(1)} %get-tuple-element.4), kind=kLoop, calls=%fused_computation | loop fusion | flops 393216 | bytes 2621440 | tf_op jit(solution)/shard_map/mul | solution.py:461
Async XLA Ops:
  0.6 34.7 %copy-start = (s32[512,256]{1,0:T(8,128)S(1)}, s32[512,256]{1,0:T(8,128)}, u32[]{:S(2)}) copy-start(s32[512,256]{1,0:T(8,128)} %coverage_hbm.1) | copy-start | bytes 1572868

commit v4 on v3

--- a/solution.py
+++ b/solution.py
@@ -108,8 +108,7 @@
             (y_weights_hbm, y_weights), (coverage_hbm, coverage), (template_var_hbm, template_var), (spread_hbm, spread),
         ))
     ]
-    for load in loads:
-        load.start()
+    loads[0].start()
 
     wide[...] = jnp.zeros_like(wide)
     near_gram[...] = jnp.zeros_like(near_gram)
@@ -123,11 +122,15 @@
     around = [((r + dr) % 4, (c + dc) % 32) for dr, dc in DIRECTIONS]
     for other in around + across + along:
         pl.semaphore_signal(barrier, inc=1, device_id=other, device_id_type=MESH)
+    for load in loads[1:]:
+        load.start()
 
     labels[pl.ds(place, 1), :] = slot[...]
     loads[0].wait()
     wide[16:528, 128:384] = template[...].astype(BF16)
     pl.semaphore_wait(barrier, 30)
+    for other in along:
+        pl.semaphore_signal(ready, inc=1, device_id=other, device_id_type=MESH)
 
     def inside(dr, dc):
         return jnp.logical_and(
@@ -200,8 +203,6 @@
             device_id_type=MESH,
         )
 
-    for other in along:
-        pl.semaphore_signal(ready, inc=1, device_id=other, device_id_type=MESH)
     for other in across:
         label_copy(place, 1, *other, 0).start()
 
@@ -211,17 +212,13 @@
     loads[1].wait()
     loads[2].wait()
 
-    def pack(number, carry):
+    def chunk(number):
         block = within(table_in[0, number])
-        send[number] = jnp.concatenate([flux[block], noise[block]], 0).astype(BF16)
-        return carry
-
-    lax.fori_loop(0, 128, pack, 0, unroll=4)
-    recv[place] = send[me]
-    pl.semaphore_wait(ready, 7)
+        return jnp.concatenate([flux[block], noise[block]], 0).astype(BF16)
 
     def send_part(step, carry):
         other = lax.rem(me + step, 128)
+        send[other] = chunk(other)
         pltpu.make_async_remote_copy(
             src_ref=send.at[other],
             dst_ref=recv.at[place],
@@ -232,7 +229,10 @@
         ).start()
         return carry
 
-    lax.fori_loop(1, 128, send_part, 0)
+    recv[place] = chunk(me)
+    pl.semaphore_wait(ready, 7)
+    lax.fori_loop(1, 127, send_part, 0, unroll=6)
+    send_part(127, 0)
 
     each_received(halo)
 
@@ -282,12 +282,15 @@
         along_y(pl.multiple_of(number * BLOCK, 16), BLOCK)
         return carry
 
-    lax.fori_loop(0, 5, y_block, 0, unroll=True)
-    along_y(480, 32)
-
+    lax.fori_loop(0, 4, y_block, 0, unroll=True)
     label_wait(112, 1)
     row_index[...] = jnp.broadcast_to(inverse_row(labels[...]), (8, 128))
-    pltpu.sync_copy(row_index, table_out)
+    table_copy = pltpu.make_async_copy(row_index, table_out, load_in.at[0])
+    table_copy.start()
+    y_block(4, 0)
+    along_y(480, 32)
+
+    table_copy.wait()
     parts = recv.at[pl.ds(0, 127)]
     pltpu.make_async_copy(parts, parts, part_in).wait()
     pltpu.make_async_copy(parts, parts, part_out).wait()

time: 36.9 us -> 37.9 us (1.027)
  Pallas kernels: 34.7 us -> 35.7 us
    pallas_call x1, Pallas kernels: 34.7 us -> 35.7 us  [local(): pl.pallas_call(kernel, out_shape=[pltpu.VMEM((512, 256), F32)] * 2, in_sp...]
where the time goes in v4:
time: 37.9 us; the launch traced here: 37.4 us
  Pallas kernels  35.7 us (94%)
  other arithmetic  1.07 us (3%)
  between operations  0.66 us (2%)
    pallas_call x1, Pallas kernels, local(): pl.pallas_call(kernel, out_shape=[pltpu.VMEM((512, 256), F32)] * 2, in_sp...  35.7 us
    mul x1, other arithmetic, local(): return (mask * residual, mask * spread_var)  1.07 us

profile of v4, /device:TPU:1, one launch (start us, length us, event | category | flops | bytes accessed | tf_op | source)
XLA Modules:
  0.0 37.4 jit_solution(1306751075788013813)
XLA Ops:
  0.6 0.0 copy-start
  0.6 35.7 %shard_map.122 = (f32[512,256]{1,0:T(8,128)S(1)}, f32[512,256]{1,0:T(8,128)S(1)}) custom-call(f32[512,256]{1,0:T(8,128)} %template_hbm.1, f32[512,256]{1,0:T(8,128)} %template_var_hbm.1, s32[512,256]{1,0:T(8,128)} %coverage_hbm.1, f32[128,8,128]{2,1,0:T(8,128)} %bitcast.10, f32[128,8,128]{2,1,0:T(8,128)} %bitcast.11, ...), custom_call_target="tpu_custom_call" | custom-call | flops 10000000000 | bytes 8000000 | tf_op jit(solution)/shard_map/pallas_call | solution.py:425
  36.3 0.0 copy-done
  36.3 1.1 %convert_multiply_fusion = (f32[512,256]{1,0:T(8,128)}, f32[512,256]{1,0:T(8,128)}) fusion(f32[512,256]{1,0:T(8,128)S(1)} %get-tuple-element.5, s32[512,256]{1,0:T(8,128)S(1)} %copy-done, f32[512,256]{1,0:T(8,128)S(1)} %get-tuple-element.4), kind=kLoop, calls=%fused_computation | loop fusion | flops 393216 | bytes 2621440 | tf_op jit(solution)/shard_map/mul | solution.py:464
Async XLA Ops:
  0.6 35.7 %copy-start = (s32[512,256]{1,0:T(8,128)S(1)}, s32[512,256]{1,0:T(8,128)}, u32[]{:S(2)}) copy-start(s32[512,256]{1,0:T(8,128)} %coverage_hbm.1) | copy-start | bytes 1572868

commit v5 on v4

--- a/solution.py
+++ b/solution.py
@@ -90,7 +90,7 @@
     owner, slot, power,
     residual, spread_var,
     template, template_var, coverage, flux, noise, x_weights, y_weights, spread,
-    wide, filtered, conv, send, recv, labels, science, science_var, root, own_gram, near_gram,
+    side_out, side_in, wide, filtered, conv, send, recv, labels, science, science_var, root, own_gram, near_gram,
     row_index, table_in, table_out,
     halo_out, halo_in, part_out, part_in, label_out, label_in, gram_out, gram_in, load_in, ready,
 ):
@@ -112,6 +112,7 @@
 
     wide[...] = jnp.zeros_like(wide)
     near_gram[...] = jnp.zeros_like(near_gram)
+    side_in[...] = jnp.zeros_like(side_in)
     own_gram[...] = jnp.zeros_like(own_gram)
 
     def column(dx, dz, dk):
@@ -125,9 +126,25 @@
     for load in loads[1:]:
         load.start()
 
+    owners = jnp.transpose(jnp.broadcast_to(owner[...], (128, 128)))
+    row_index[...] = jnp.broadcast_to(inverse_row(owners), (8, 128))
+    owner_copy = pltpu.make_async_copy(row_index, table_in, load_in.at[8])
+    owner_copy.start()
     labels[pl.ds(place, 1), :] = slot[...]
     loads[0].wait()
     wide[16:528, 128:384] = template[...].astype(BF16)
+    side_row = lax.broadcasted_iota(jnp.int32, (16, 128), 0)
+    side_lane = lax.broadcasted_iota(jnp.int32, (16, 128), 1)
+    sides = [
+        jnp.where(side_lane == side_row + first, 1.0, 0.0).astype(BF16) for first in (0, 112)
+    ]
+    for number in range(2):
+        side_out[number] = lax.dot_general(
+            sides[number],
+            wide[16:528, 128 + 128 * number : 256 + 128 * number],
+            (((1,), (1,)), ((), ())),
+            preferred_element_type=F32,
+        ).astype(BF16)
     pl.semaphore_wait(barrier, 30)
     for other in along:
         pl.semaphore_signal(ready, inc=1, device_id=other, device_id_type=MESH)
@@ -148,8 +165,8 @@
     def halo(number):
         dr, dc = DIRECTIONS[number]
         return pltpu.make_async_remote_copy(
-            src_ref=wide.at[source_rows[dr], source_cols[dc]],
-            dst_ref=wide.at[target_rows[dr], target_cols[dc]],
+            src_ref=wide.at[source_rows[dr], source_cols[dc]] if dr else side_out.at[number],
+            dst_ref=wide.at[target_rows[dr], target_cols[dc]] if dr else side_in.at[number],
             send_sem=halo_out.at[number],
             recv_sem=halo_in.at[number],
             device_id=target(dr, dc),
@@ -206,9 +223,7 @@
     for other in across:
         label_copy(place, 1, *other, 0).start()
 
-    owners = jnp.transpose(jnp.broadcast_to(owner[...], (128, 128)))
-    row_index[...] = jnp.broadcast_to(inverse_row(owners), (8, 128))
-    pltpu.sync_copy(row_index, table_in)
+    owner_copy.wait()
     loads[1].wait()
     loads[2].wait()
 
@@ -216,25 +231,46 @@
         block = within(table_in[0, number])
         return jnp.concatenate([flux[block], noise[block]], 0).astype(BF16)
 
-    def send_part(step, carry):
-        other = lax.rem(me + step, 128)
-        send[other] = chunk(other)
-        pltpu.make_async_remote_copy(
-            src_ref=send.at[other],
-            dst_ref=recv.at[place],
-            send_sem=part_out,
-            recv_sem=part_in,
-            device_id=(other // 32, other % 32),
-            device_id_type=MESH,
-        ).start()
+    def label_wait(count, which):
+        part = labels.at[pl.ds(0, count)]
+        pltpu.make_async_copy(part, part, label_in.at[which]).wait()
+        pltpu.make_async_copy(part, part, label_out.at[which]).wait()
+
+    def send_to(others):
+        for row, col in others:
+            send[row * 32 + col] = chunk(row * 32 + col)
+        for row, col in others:
+            pltpu.make_async_remote_copy(
+                src_ref=send.at[row * 32 + col],
+                dst_ref=recv.at[place],
+                send_sem=part_out,
+                recv_sem=part_in,
+                device_id=(row, col),
+                device_id_type=MESH,
+            ).start()
+
+    def send_group(group, carry):
+        send_to([
+            ((r + group // 4) % 4, column(group % 4, dz, dk)) for dz in range(4) for dk in range(2) if dz or dk
+        ])
         return carry
 
     recv[place] = chunk(me)
+    send_to(across)
+    send_to(along)
     pl.semaphore_wait(ready, 7)
-    lax.fori_loop(1, 127, send_part, 0, unroll=6)
-    send_part(127, 0)
+    lax.fori_loop(1, 8, send_group, 0)
+    label_wait(15, 0)
+    for other in along:
+        label_copy(pl.multiple_of((z * 2 + k) * 16, 16), 16, *other, 1).start()
+    lax.fori_loop(8, 16, send_group, 0)
 
     each_received(halo)
+
+    for number in range(2):
+        wide[16:528, 384 - 384 * number : 512 - 384 * number] = lax.dot_general(
+            side_in[number], sides[number], (((0,), (0,)), ((), ())), preferred_element_type=F32
+        ).astype(BF16)
 
     filtered[:, 544:608, :] = jnp.zeros((16, 64, 256), BF16)
     loads[3].wait()
@@ -251,15 +287,6 @@
         return carry
 
     lax.fori_loop(0, 8, along_x, 0, unroll=True)
-
-    def label_wait(count, which):
-        part = labels.at[pl.ds(0, count)]
-        pltpu.make_async_copy(part, part, label_in.at[which]).wait()
-        pltpu.make_async_copy(part, part, label_out.at[which]).wait()
-
-    label_wait(15, 0)
-    for other in along:
-        label_copy(pl.multiple_of((z * 2 + k) * 16, 16), 16, *other, 1).start()
 
     def along_y(first, rows):
         for pair in range(3):
@@ -436,6 +463,8 @@
             pltpu.VMEM((8, 256, 256), BF16),
             pltpu.VMEM((8, BLOCK * 8, 256), BF16),
             pltpu.VMEM((2, 128, 768), BF16),
+            pltpu.VMEM((2, 16, 512), BF16),
+            pltpu.VMEM((2, 16, 512), BF16),
             pltpu.VMEM((544, 512), BF16),
             pltpu.VMEM((16, 608, 256), BF16),
             pltpu.VMEM((512, 48, 256), BF16),
@@ -450,7 +479,7 @@
             pltpu.VMEM((8, 128), jnp.int32),
             pltpu.SMEM((8, 128), jnp.int32),
             pltpu.SMEM((8, 128), jnp.int32),
-            dma((8,)), dma((8,)), dma, dma, dma((2,)), dma((2,)), dma((10,)), dma((10,)), dma((8,)), pltpu.SemaphoreType.REGULAR,
+            dma((8,)), dma((8,)), dma, dma, dma((2,)), dma((2,)), dma((10,)), dma((10,)), dma((9,)), pltpu.SemaphoreType.REGULAR,
         ],
         compiler_params=pltpu.CompilerParams(
             collective_id=0, has_side_effects=True, vmem_limit_bytes=60 * 1024 * 1024

time: 37.9 us -> 35.8 us (0.945); the launches traced: 37.4 us -> 35.7 us
  Pallas kernels: 35.7 us -> 34 us
    pallas_call x1, Pallas kernels: 35.7 us -> 34 us  [local(): pl.pallas_call(kernel, out_shape=[pltpu.VMEM((512, 256), F32)] * 2, in_sp...]
where the time goes in v5:
time: 35.8 us; the launch traced here: 35.7 us
  Pallas kernels  34 us (95%)
  other arithmetic  1.07 us (3%)
  between operations  0.66 us (2%)
    pallas_call x1, Pallas kernels, local(): pl.pallas_call(kernel, out_shape=[pltpu.VMEM((512, 256), F32)] * 2, in_sp...  34 us
    mul x1, other arithmetic, local(): return (mask * residual, mask * spread_var)  1.07 us

profile of v5, /device:TPU:1, one launch (start us, length us, event | category | flops | bytes accessed | tf_op | source)
XLA Modules:
  0.0 35.7 jit_solution(4680851057316458472)
XLA Ops:
  0.6 0.0 copy-start
  0.6 34.0 %shard_map.122 = (f32[512,256]{1,0:T(8,128)S(1)}, f32[512,256]{1,0:T(8,128)S(1)}) custom-call(f32[512,256]{1,0:T(8,128)} %template_hbm.1, f32[512,256]{1,0:T(8,128)} %template_var_hbm.1, s32[512,256]{1,0:T(8,128)} %coverage_hbm.1, f32[128,8,128]{2,1,0:T(8,128)} %bitcast.10, f32[128,8,128]{2,1,0:T(8,128)} %bitcast.11, ...), custom_call_target="tpu_custom_call" | custom-call | flops 10000000000 | bytes 8000000 | tf_op jit(solution)/shard_map/pallas_call | solution.py:452
  34.6 0.0 copy-done
  34.6 1.1 %convert_multiply_fusion = (f32[512,256]{1,0:T(8,128)}, f32[512,256]{1,0:T(8,128)}) fusion(f32[512,256]{1,0:T(8,128)S(1)} %get-tuple-element.5, s32[512,256]{1,0:T(8,128)S(1)} %copy-done, f32[512,256]{1,0:T(8,128)S(1)} %get-tuple-element.4), kind=kLoop, calls=%fused_computation | loop fusion | flops 393216 | bytes 2621440 | tf_op jit(solution)/shard_map/mul | solution.py:493
Async XLA Ops:
  0.6 34.0 %copy-start = (s32[512,256]{1,0:T(8,128)S(1)}, s32[512,256]{1,0:T(8,128)}, u32[]{:S(2)}) copy-start(s32[512,256]{1,0:T(8,128)} %coverage_hbm.1) | copy-start | bytes 1572868

commit v6 on v5

--- a/solution.py
+++ b/solution.py
@@ -92,7 +92,7 @@
     template, template_var, coverage, flux, noise, x_weights, y_weights, spread,
     side_out, side_in, wide, filtered, conv, send, recv, labels, science, science_var, root, own_gram, near_gram,
     row_index, table_in, table_out,
-    halo_out, halo_in, part_out, part_in, label_out, label_in, gram_out, gram_in, load_in, ready,
+    halo_out, halo_in, part_out, part_in, label_out, label_in, gram_out, gram_in, load_in, ready, blend,
 ):
     r = lax.axis_index("row")
     c = lax.axis_index("col")
@@ -332,7 +332,7 @@
         science_var[rows, 128:256] = jnp.concatenate([upper[12:16], lower[12:16]], 0)
         return carry
 
-    lax.fori_loop(0, 64, unpack, 0, unroll=4)
+    lax.fori_loop(0, 64, unpack, 0, unroll=8)
     loads[5].wait()
     root[...] = coverage[...].astype(F32) * lax.rsqrt(science_var[...])
 
@@ -422,20 +422,19 @@
     loads[6].wait()
     loads[7].wait()
     for patch in range(2):
-        coefficients = jnp.where(
+        blend[patch] = jnp.where(
             chosen, jnp.dot(both, spread[patch], preferred_element_type=F32), 0.0
         ).astype(BF16)
-        kernel_power = powers[patch]
-
-        def finish(number, carry):
-            rows = pl.ds(pl.multiple_of(number * 16, 16), 16)
-            product = jnp.dot(coefficients, conv[rows].reshape(768, 256), preferred_element_type=F32)
-            model = product[0:16] + product[16:32]
-            residual[rows] = science[rows] - model
-            spread_var[rows] = science_var[rows] + kernel_power * template_var[rows]
-            return carry
-
-        lax.fori_loop(16 * patch, 16 * patch + 16, finish, 0, unroll=8)
+
+    def finish(number, carry):
+        rows = pl.ds(pl.multiple_of(number * 16, 16), 16)
+        product = jnp.dot(blend[number // 16], conv[rows].reshape(768, 256), preferred_element_type=F32)
+        residual[rows] = science[rows] - (product[0:16] + product[16:32])
+        kernel_power = jnp.where(number < 16, powers[0], powers[1])
+        spread_var[rows] = science_var[rows] + kernel_power * template_var[rows]
+        return carry
+
+    lax.fori_loop(0, 32, finish, 0, unroll=16)
 
     each_sent(halo, lambda copy: copy.wait_send())
     grams_sent(lambda copy: copy.wait_send())
@@ -480,6 +479,7 @@
             pltpu.SMEM((8, 128), jnp.int32),
             pltpu.SMEM((8, 128), jnp.int32),
             dma((8,)), dma((8,)), dma, dma, dma((2,)), dma((2,)), dma((10,)), dma((10,)), dma((9,)), pltpu.SemaphoreType.REGULAR,
+            pltpu.VMEM((2, 32, 768), BF16),
         ],
         compiler_params=pltpu.CompilerParams(
             collective_id=0, has_side_effects=True, vmem_limit_bytes=60 * 1024 * 1024

time: 35.8 us -> 35.5 us (level)
  Pallas kernels: 34 us -> 33.6 us
    pallas_call x1, Pallas kernels: 34 us -> 33.6 us  [local(): pl.pallas_call(kernel, out_shape=[pltpu.VMEM((512, 256), F32)] * 2, in_sp...]
where the time goes in v6:
time: 35.5 us; the launch traced here: 35.3 us
  Pallas kernels  33.6 us (95%)
  other arithmetic  1.07 us (3%)
  between operations  0.66 us (2%)
    pallas_call x1, Pallas kernels, local(): pl.pallas_call(kernel, out_shape=[pltpu.VMEM((512, 256), F32)] * 2, in_sp...  33.6 us
    mul x1, other arithmetic, local(): return (mask * residual, mask * spread_var)  1.07 us

profile of v6, /device:TPU:1, one launch (start us, length us, event | category | flops | bytes accessed | tf_op | source)
XLA Modules:
  0.0 35.3 jit_solution(16566287504936176474)
XLA Ops:
  0.6 0.0 copy-start
  0.6 33.6 %shard_map.122 = (f32[512,256]{1,0:T(8,128)S(1)}, f32[512,256]{1,0:T(8,128)S(1)}) custom-call(f32[512,256]{1,0:T(8,128)} %template_hbm.1, f32[512,256]{1,0:T(8,128)} %template_var_hbm.1, s32[512,256]{1,0:T(8,128)} %coverage_hbm.1, f32[128,8,128]{2,1,0:T(8,128)} %bitcast.10, f32[128,8,128]{2,1,0:T(8,128)} %bitcast.11, ...), custom_call_target="tpu_custom_call" | custom-call | flops 10000000000 | bytes 8000000 | tf_op jit(solution)/shard_map/pallas_call | solution.py:451
  34.3 0.0 copy-done
  34.3 1.1 %convert_multiply_fusion = (f32[512,256]{1,0:T(8,128)}, f32[512,256]{1,0:T(8,128)}) fusion(f32[512,256]{1,0:T(8,128)S(1)} %get-tuple-element.5, s32[512,256]{1,0:T(8,128)S(1)} %copy-done, f32[512,256]{1,0:T(8,128)S(1)} %get-tuple-element.4), kind=kLoop, calls=%fused_computation | loop fusion | flops 393216 | bytes 2621440 | tf_op jit(solution)/shard_map/mul | solution.py:493
Async XLA Ops:
  0.6 33.6 %copy-start = (s32[512,256]{1,0:T(8,128)S(1)}, s32[512,256]{1,0:T(8,128)}, u32[]{:S(2)}) copy-start(s32[512,256]{1,0:T(8,128)} %coverage_hbm.1) | copy-start | bytes 1572868

commit v7 on v6

--- a/solution.py
+++ b/solution.py
@@ -120,7 +120,7 @@
 
     across = [((r + dr) % 4, column(dx, 0, 0)) for dr in range(4) for dx in range(4) if dr or dx]
     along = [(r, column(0, dz, dk)) for dz in range(4) for dk in range(2) if dz or dk]
-    around = [((r + dr) % 4, (c + dc) % 32) for dr, dc in DIRECTIONS]
+    around = [((r + dr) % 4, (c + dc) % 32) for dr, dc in DIRECTIONS if dc]
     for other in around + across + along:
         pl.semaphore_signal(barrier, inc=1, device_id=other, device_id_type=MESH)
     for load in loads[1:]:
@@ -145,7 +145,7 @@
             (((1,), (1,)), ((), ())),
             preferred_element_type=F32,
         ).astype(BF16)
-    pl.semaphore_wait(barrier, 30)
+    pl.semaphore_wait(barrier, 28)
     for other in along:
         pl.semaphore_signal(ready, inc=1, device_id=other, device_id_type=MESH)
 
@@ -320,7 +320,6 @@
     table_copy.wait()
     parts = recv.at[pl.ds(0, 127)]
     pltpu.make_async_copy(parts, parts, part_in).wait()
-    pltpu.make_async_copy(parts, parts, part_out).wait()
 
     def unpack(number, carry):
         upper = recv[within(table_out[0, 2 * number])].astype(F32)
@@ -438,6 +437,7 @@
 
     each_sent(halo, lambda copy: copy.wait_send())
     grams_sent(lambda copy: copy.wait_send())
+    pltpu.make_async_copy(parts, parts, part_out).wait()
 
 
 def local(template, template_var, coverage, exposure, exposure_var, strip_owner, strip_slot):

time: 35.5 us -> 35.4 us (level)
  no operation moved by 1% of the time
where the time goes in v7:
time: 35.4 us; the launch traced here: 35.3 us
  Pallas kernels  33.6 us (95%)
  other arithmetic  1.07 us (3%)
  between operations  0.66 us (2%)
    pallas_call x1, Pallas kernels, local(): pl.pallas_call(kernel, out_shape=[pltpu.VMEM((512, 256), F32)] * 2, in_sp...  33.6 us
    mul x1, other arithmetic, local(): return (mask * residual, mask * spread_var)  1.07 us

profile of v7, /device:TPU:1, one launch (start us, length us, event | category | flops | bytes accessed | tf_op | source)
XLA Modules:
  0.0 35.3 jit_solution(243871497424475161)
XLA Ops:
  0.6 0.0 copy-start
  0.6 33.6 %shard_map.122 = (f32[512,256]{1,0:T(8,128)S(1)}, f32[512,256]{1,0:T(8,128)S(1)}) custom-call(f32[512,256]{1,0:T(8,128)} %template_hbm.1, f32[512,256]{1,0:T(8,128)} %template_var_hbm.1, s32[512,256]{1,0:T(8,128)} %coverage_hbm.1, f32[128,8,128]{2,1,0:T(8,128)} %bitcast.10, f32[128,8,128]{2,1,0:T(8,128)} %bitcast.11, ...), custom_call_target="tpu_custom_call" | custom-call | flops 10000000000 | bytes 8000000 | tf_op jit(solution)/shard_map/pallas_call | solution.py:451
  34.2 0.0 copy-done
  34.2 1.1 %convert_multiply_fusion = (f32[512,256]{1,0:T(8,128)}, f32[512,256]{1,0:T(8,128)}) fusion(f32[512,256]{1,0:T(8,128)S(1)} %get-tuple-element.5, s32[512,256]{1,0:T(8,128)S(1)} %copy-done, f32[512,256]{1,0:T(8,128)S(1)} %get-tuple-element.4), kind=kLoop, calls=%fused_computation | loop fusion | flops 393216 | bytes 2621440 | tf_op jit(solution)/shard_map/mul | solution.py:493
Async XLA Ops:
  0.6 33.6 %copy-start = (s32[512,256]{1,0:T(8,128)S(1)}, s32[512,256]{1,0:T(8,128)}, u32[]{:S(2)}) copy-start(s32[512,256]{1,0:T(8,128)} %coverage_hbm.1) | copy-start | bytes 1572868

commit v8 on v7

--- a/solution.py
+++ b/solution.py
@@ -327,13 +327,17 @@
         rows = pl.ds(pl.multiple_of(number * 8, 8), 8)
         science[rows, 0:128] = jnp.concatenate([upper[0:4], lower[0:4]], 0)
         science[rows, 128:256] = jnp.concatenate([upper[4:8], lower[4:8]], 0)
-        science_var[rows, 0:128] = jnp.concatenate([upper[8:12], lower[8:12]], 0)
-        science_var[rows, 128:256] = jnp.concatenate([upper[12:16], lower[12:16]], 0)
+        for side in range(2):
+            lanes = pl.ds(128 * side, 128)
+            part = slice(8 + 4 * side, 12 + 4 * side)
+            noise_rows = jnp.concatenate([upper[part], lower[part]], 0)
+            science_var[rows, lanes] = noise_rows
+            root[rows, lanes] = coverage[rows, lanes].astype(F32) * lax.rsqrt(noise_rows)
         return carry
 
+    loads[5].wait()
+
     lax.fori_loop(0, 64, unpack, 0, unroll=8)
-    loads[5].wait()
-    root[...] = coverage[...].astype(F32) * lax.rsqrt(science_var[...])
 
     is_target = lax.broadcasted_iota(jnp.int32, (16, 256), 0) == TARGET - 32
 

time: 35.4 us -> 35.4 us (level)
  no operation moved by 1% of the time
where the time goes in v8:
time: 35.4 us; the launch traced here: 35.3 us
  Pallas kernels  33.5 us (95%)
  other arithmetic  1.07 us (3%)
  between operations  0.66 us (2%)
    pallas_call x1, Pallas kernels, local(): pl.pallas_call(kernel, out_shape=[pltpu.VMEM((512, 256), F32)] * 2, in_sp...  33.5 us
    mul x1, other arithmetic, local(): return (mask * residual, mask * spread_var)  1.07 us

profile of v8, /device:TPU:1, one launch (start us, length us, event | category | flops | bytes accessed | tf_op | source)
XLA Modules:
  0.0 35.3 jit_solution(16658382757152338262)
XLA Ops:
  0.6 0.0 copy-start
  0.6 33.5 %shard_map.122 = (f32[512,256]{1,0:T(8,128)S(1)}, f32[512,256]{1,0:T(8,128)S(1)}) custom-call(f32[512,256]{1,0:T(8,128)} %template_hbm.1, f32[512,256]{1,0:T(8,128)} %template_var_hbm.1, s32[512,256]{1,0:T(8,128)} %coverage_hbm.1, f32[128,8,128]{2,1,0:T(8,128)} %bitcast.10, f32[128,8,128]{2,1,0:T(8,128)} %bitcast.11, ...), custom_call_target="tpu_custom_call" | custom-call | flops 10000000000 | bytes 8000000 | tf_op jit(solution)/shard_map/pallas_call | solution.py:455
  34.2 0.0 copy-done
  34.2 1.1 %convert_multiply_fusion = (f32[512,256]{1,0:T(8,128)}, f32[512,256]{1,0:T(8,128)}) fusion(f32[512,256]{1,0:T(8,128)S(1)} %get-tuple-element.5, s32[512,256]{1,0:T(8,128)S(1)} %copy-done, f32[512,256]{1,0:T(8,128)S(1)} %get-tuple-element.4), kind=kLoop, calls=%fused_computation | loop fusion | flops 393216 | bytes 2621440 | tf_op jit(solution)/shard_map/mul | solution.py:497
Async XLA Ops:
  0.6 33.5 %copy-start = (s32[512,256]{1,0:T(8,128)S(1)}, s32[512,256]{1,0:T(8,128)}, u32[]{:S(2)}) copy-start(s32[512,256]{1,0:T(8,128)} %coverage_hbm.1) | copy-start | bytes 1572868
